TPU v7x, 32 devices: a whole 2x2x4 slice. The times are simulated.
32 devices in a mesh: dp: 8 (over z, x), tensor: 4 (over y, core).
Axes of the slice: x: 2, y: 2, z: 4, core: 2. Of those that a mesh axis runs over, the one named last changes fastest.
Arguments:
- hidden_in: bfloat16 [24576, 1024], P(('dp', 'tensor')), may hold values from -6 to 6
- segments: int32 [24576], P('dp'), may hold values from 0 to 80, never falling along the last dimension, each value on 1 to 800 neighbouring positions
- cotangent: bfloat16 [24576, 1024], P(('dp', 'tensor')), may hold values from -6 to 6
- w_z: bfloat16 [1024, 2048], P('dp', 'tensor'), may hold values from -0.1875 to 0.1875
- w_x: bfloat16 [1024, 2048], P('dp', 'tensor'), may hold values from -0.1875 to 0.1875
- w_bc: bfloat16 [1024, 256], P('dp'), may hold values from -0.1875 to 0.1875
- w_dt: bfloat16 [1024, 32], P('dp', 'tensor'), may hold values from -0.1875 to 0.1875
- w_out: bfloat16 [2048, 1024], P('tensor', 'dp'), may hold values from -0.125 to 0.125
- norm_gain: bfloat16 [1024], P('dp'), may hold values from 0.5 to 1.5
- conv_x: bfloat16 [4, 32, 64], P(None, 'tensor', 'dp'), may hold values from -3 to 3
- bias_x: bfloat16 [32, 64], P('tensor', 'dp'), may hold values from -2 to 2
- conv_bc: bfloat16 [4, 256], P(None, 'dp'), may hold values from -3 to 3
- bias_bc: bfloat16 [256], P('dp'), may hold values from -2 to 2
- gate_gain: bfloat16 [32, 64], P('tensor', 'dp'), may hold values from 0.5 to 1.5
- dt_bias: float32 [32], P('tensor'), may hold values from -6.9 to -2.3
- a_log: float32 [32], P('tensor'), may hold values from 0 to 2.77
- d_skip: float32 [32], P('tensor'), may hold values from 0.5 to 1.5
Outputs:
- block_out: bfloat16 [24576, 1024], P(('dp', 'tensor'))
- grad_hidden: float32 [24576, 1024], P(('dp', 'tensor'))
- grad_w_z: float32 [1024, 2048], P('dp', 'tensor')
- grad_w_x: float32 [1024, 2048], P('dp', 'tensor')
- grad_w_bc: float32 [1024, 256], P('dp')
- grad_w_dt: float32 [1024, 32], P('dp', 'tensor')
- grad_w_out: float32 [2048, 1024], P('tensor', 'dp')
- grad_norm_gain: float32 [1024], P('dp')
- grad_conv_x: float32 [4, 32, 64], P(None, 'tensor', 'dp')
- grad_bias_x: float32 [32, 64], P('tensor', 'dp')
- grad_conv_bc: float32 [4, 256], P(None, 'dp')
- grad_bias_bc: float32 [256], P('dp')
- grad_gate_gain: float32 [32, 64], P('tensor', 'dp')
- grad_dt_bias: float32 [32], P('tensor')
- grad_a_log: float32 [32], P('tensor')
- grad_d_skip: float32 [32], P('tensor')
Inputs may be any that keep to these rules, and one draw needn't show every extreme that they name: `segments`: segment numbers never fall along the tokens; a document holds 1 to 800 tokens and one holds exactly 800.
All inputs are finite; a program needn't handle non-finite values.
Results may differ from a plain program's by a relative error of at most 0.0085.
Values may be sent and summed in bfloat16 or wider, within the bound.
A program may use at most 192 MiB of HBM per device.

v0:
```python
import jax
import jax.numpy as jnp
from jax import lax
from jax.sharding import PartitionSpec as P

BLOCK = 256
SEQ_LEN = 1024


EPSILON = 1e-05
HIGHEST = lax.Precision.HIGHEST


def causal_conv(inputs, filters, shifts, doc_rows):
    tap_count = filters.shape[0]
    summed = shifts + filters[tap_count - 1] * inputs
    for offset in range(1, tap_count):
        shifted = jnp.pad(inputs, ((0, 0), (offset, 0), (0, 0)))[:, :-offset]
        shifted_doc = jnp.pad(doc_rows, ((0, 0), (offset, 0)), constant_values=-1)[:, :-offset]
        same_doc = (shifted_doc == doc_rows).astype(inputs.dtype)
        summed = summed + filters[tap_count - 1 - offset] * shifted * same_doc[:, :, None]
    return summed


def scan_sequence(values, b_rows, c_rows, step_sizes, decay_rates, skip_gain, doc_ids, block_len):
    length, head_count, head_width = values.shape
    blocks_count = length // block_len
    value_blocks = values.reshape(blocks_count, block_len, head_count, head_width)
    b_blocks = b_rows.reshape(blocks_count, block_len, -1)
    c_blocks = c_rows.reshape(blocks_count, block_len, -1)
    step_blocks = jnp.transpose(step_sizes.reshape(blocks_count, block_len, head_count), (0, 2, 1))
    doc_blocks = doc_ids.reshape(blocks_count, block_len)
    cumulative = jnp.cumsum(step_blocks * decay_rates[None, :, None], axis=2)
    positions = jnp.arange(block_len)
    causal = positions[:, None] >= positions[None, :]
    same_doc = (doc_blocks[:, :, None] == doc_blocks[:, None, :]) & causal[None]
    mask_float = same_doc.astype(values.dtype)[:, None]
    spread = cumulative[:, :, :, None] - cumulative[:, :, None, :]
    decays = jnp.exp(spread * mask_float) * mask_float
    scores = jnp.einsum("ctn,csn->cts", c_blocks, b_blocks, precision=HIGHEST)
    weights = decays * scores[:, None] * step_blocks[:, :, None, :]
    intra_out = jnp.einsum("chts,cshp->cthp", weights, value_blocks, precision=HIGHEST)
    last_doc = doc_blocks[:, -1]
    tail_mask = (doc_blocks == last_doc[:, None]).astype(values.dtype)
    to_end = jnp.exp(cumulative[:, :, -1:] - cumulative) * tail_mask[:, None, :] * step_blocks
    local_states = jnp.einsum(
        "csn,chs,cshp->chnp", b_blocks, to_end, value_blocks, precision=HIGHEST
    )
    carry_state = local_states[0]
    pieces = [intra_out[0]]
    for block_index in range(1, blocks_count):
        reach_mask = (doc_blocks[block_index] == last_doc[block_index - 1]).astype(values.dtype)
        entry_decay = jnp.exp(cumulative[block_index]) * reach_mask[None, :]
        carried = jnp.einsum("tn,hnp->thp", c_blocks[block_index], carry_state, precision=HIGHEST)
        pieces.append(intra_out[block_index] + carried * jnp.transpose(entry_decay)[:, :, None])
        keep_state = (last_doc[block_index] == last_doc[block_index - 1]).astype(values.dtype)
        carry_state = (
            local_states[block_index]
            + (keep_state * jnp.exp(cumulative[block_index, :, -1]))[:, None, None] * carry_state
        )
    result = jnp.stack(pieces).reshape(length, head_count, head_width)
    return result + skip_gain[None, :, None] * values


def mixer(
    proj_x,
    proj_bc,
    proj_dt,
    conv_x,
    bias_x,
    conv_bc,
    bias_bc,
    dt_bias,
    a_log,
    d_skip,
    doc_ids,
    seq_len,
    block_len,
):
    tokens_count = proj_x.shape[0]
    seq_count = tokens_count // seq_len
    head_count = proj_dt.shape[1]
    head_width = proj_x.shape[1] // head_count
    state_size = proj_bc.shape[1] // 2
    doc_rows = doc_ids.reshape(seq_count, seq_len)
    filter_x = conv_x.reshape(conv_x.shape[0], -1)
    x_conv = jax.nn.silu(
        causal_conv(proj_x.reshape(seq_count, seq_len, -1), filter_x, bias_x.reshape(-1), doc_rows)
    )
    bc_conv = jax.nn.silu(
        causal_conv(proj_bc.reshape(seq_count, seq_len, -1), conv_bc, bias_bc, doc_rows)
    )
    step_sizes = jax.nn.softplus(proj_dt + dt_bias).reshape(seq_count, seq_len, head_count)
    decay_rates = -jnp.exp(a_log)

    def one_sequence(seq_item):
        x_seq, bc_seq, dt_seq, doc_seq = seq_item
        out_seq = scan_sequence(
            x_seq.reshape(seq_len, head_count, head_width),
            bc_seq[:, :state_size],
            bc_seq[:, state_size:],
            dt_seq,
            decay_rates,
            d_skip,
            doc_seq,
            block_len,
        )
        return out_seq.reshape(seq_len, head_count * head_width)

    mixed = lax.map(jax.checkpoint(one_sequence), (x_conv, bc_conv, step_sizes, doc_rows))
    return mixed.reshape(tokens_count, head_count * head_width)


def times_trans(left, right):
    return lax.dot_general(
        left, right, (((1,), (1,)), ((), ())), preferred_element_type=jnp.float32
    )


def trans_times(left, right):
    return lax.dot_general(
        left, right, (((0,), (0,)), ((), ())), preferred_element_type=jnp.float32
    )


def shards(
    hidden_in,
    segments,
    cotangent,
    w_z,
    w_x,
    w_bc,
    w_dt,
    w_out,
    norm_gain,
    conv_x,
    bias_x,
    conv_bc,
    bias_bc,
    gate_gain,
    dt_bias,
    a_log,
    d_skip,
):
    (
        proj_z,
        proj_x,
        proj_bc,
        proj_dt,
        proj_out,
        gain_in,
        filter_x,
        shift_x,
        filter_bc,
        shift_bc,
        gain_gate,
    ) = (
        lax.all_gather(w_z, "dp", axis=0, tiled=True),
        lax.all_gather(w_x, "dp", axis=0, tiled=True),
        lax.all_gather(w_bc, "dp", axis=0, tiled=True),
        lax.all_gather(w_dt, "dp", axis=0, tiled=True),
        lax.all_gather(w_out, "dp", axis=1, tiled=True),
        lax.all_gather(norm_gain, "dp", axis=0, tiled=True),
        lax.all_gather(conv_x, "dp", axis=2, tiled=True),
        lax.all_gather(bias_x, "dp", axis=1, tiled=True),
        lax.all_gather(conv_bc, "dp", axis=1, tiled=True),
        lax.all_gather(bias_bc, "dp", axis=0, tiled=True),
        lax.all_gather(gate_gain, "dp", axis=1, tiled=True),
    )
    resid = hidden_in.astype(jnp.float32)
    inv_in = lax.rsqrt(jnp.mean(resid * resid, -1, keepdims=True) + EPSILON)
    normed_rows = (resid * inv_in * gain_in.astype(jnp.float32)).astype(jnp.bfloat16)
    normed = lax.all_gather(normed_rows, "tensor", axis=0, tiled=True)
    gate_raw = jnp.dot(normed, proj_z, preferred_element_type=jnp.float32)
    value_raw = jnp.dot(normed, proj_x, preferred_element_type=jnp.float32)
    bc_raw = jnp.dot(normed, proj_bc, preferred_element_type=jnp.float32)
    dt_raw = jnp.dot(normed, proj_dt, preferred_element_type=jnp.float32)

    def local_mixer(
        value_in,
        bc_in,
        dt_in,
        conv_value,
        bias_value,
        conv_state,
        bias_state,
        dt_shift,
        log_rate,
        skip_gain,
    ):
        return mixer(
            value_in,
            bc_in,
            dt_in,
            conv_value,
            bias_value,
            conv_state,
            bias_state,
            dt_shift,
            log_rate,
            skip_gain,
            segments,
            SEQ_LEN,
            BLOCK,
        )

    mixed, mixer_back = jax.vjp(
        local_mixer,
        value_raw,
        bc_raw,
        dt_raw,
        filter_x.astype(jnp.float32),
        shift_x.astype(jnp.float32),
        filter_bc.astype(jnp.float32),
        shift_bc.astype(jnp.float32),
        dt_bias,
        a_log,
        d_skip,
    )
    gate_act = jax.nn.silu(gate_raw)
    gated = mixed * gate_act
    tensor_count = lax.axis_size("tensor")
    channels = gated.shape[1] * tensor_count
    square_sum = lax.psum(jnp.sum(gated * gated, -1), "tensor")
    inv_gate = lax.rsqrt(square_sum / channels + EPSILON)[:, None]
    gain_flat = gain_gate.astype(jnp.float32).reshape(-1)
    scaled = (gated * inv_gate * gain_flat).astype(jnp.bfloat16)
    scaled_own = lax.all_to_all(scaled, "tensor", split_axis=0, concat_axis=1, tiled=True)
    out_full = lax.all_gather(proj_out, "tensor", axis=0, tiled=True)
    out_rows = jnp.dot(scaled_own, out_full, preferred_element_type=jnp.float32)
    block_out = (resid + out_rows).astype(jnp.bfloat16)
    cot_float = cotangent.astype(jnp.float32)
    cot_full = lax.all_gather(cotangent, "tensor", axis=0, tiled=True)
    d_scaled = times_trans(cot_full, proj_out)
    inner = lax.psum(jnp.sum(gated * d_scaled * gain_flat, -1), "tensor")
    grad_out = trans_times(scaled, cot_full)
    grad_gate = jnp.sum(d_scaled * gated * inv_gate, 0).reshape(gain_gate.shape)
    d_gated = inv_gate * d_scaled * gain_flat - gated * inv_gate**3 * inner[:, None] / channels
    d_mixed = d_gated * gate_act
    sigma = jax.nn.sigmoid(gate_raw)
    d_gate_low = (d_gated * mixed * sigma * (1.0 + gate_raw * (1.0 - sigma))).astype(jnp.bfloat16)
    (
        d_value,
        d_bc,
        d_dt,
        grad_conv_x,
        grad_bias_x,
        grad_conv_bc,
        grad_bias_bc,
        grad_dt_shift,
        grad_log_rate,
        grad_skip,
    ) = mixer_back(d_mixed)
    d_value_low = d_value.astype(jnp.bfloat16)
    d_dt_low = d_dt.astype(jnp.bfloat16)
    d_normed_part = (
        times_trans(d_gate_low, proj_z)
        + times_trans(d_value_low, proj_x)
        + times_trans(d_dt_low, proj_dt)
    )
    d_rows, d_bc_rows = (
        lax.psum_scatter(d_normed_part, "tensor", scatter_dimension=0, tiled=True),
        lax.psum_scatter(d_bc, "tensor", scatter_dimension=0, tiled=True),
    )
    d_bc_low = d_bc_rows.astype(jnp.bfloat16)
    d_normed_rows = d_rows + times_trans(d_bc_low, proj_bc)
    grad_z = trans_times(normed, d_gate_low)
    grad_x = trans_times(normed, d_value_low)
    grad_dt = trans_times(normed, d_dt_low)
    grad_bc_part = trans_times(normed_rows, d_bc_low)
    grad_gain_part = jnp.sum(d_normed_rows * resid * inv_in, 0)
    weighted = d_normed_rows * gain_in.astype(jnp.float32)
    grad_hidden = (
        cot_float
        + inv_in * weighted
        - resid * inv_in**3 * jnp.mean(weighted * resid, -1, keepdims=True)
    )
    summed = (
        lax.psum_scatter(grad_z, "dp", scatter_dimension=0, tiled=True),
        lax.psum_scatter(grad_x, "dp", scatter_dimension=0, tiled=True),
        lax.psum_scatter(grad_bc_part, "dp", scatter_dimension=0, tiled=True),
        lax.psum_scatter(grad_dt, "dp", scatter_dimension=0, tiled=True),
        lax.psum_scatter(grad_out, "dp", scatter_dimension=1, tiled=True),
        lax.psum_scatter(grad_gain_part, "dp", scatter_dimension=0, tiled=True),
        lax.psum_scatter(grad_conv_x, "dp", scatter_dimension=2, tiled=True),
        lax.psum_scatter(grad_bias_x, "dp", scatter_dimension=1, tiled=True),
        lax.psum_scatter(grad_conv_bc, "dp", scatter_dimension=1, tiled=True),
        lax.psum_scatter(grad_bias_bc, "dp", scatter_dimension=0, tiled=True),
        lax.psum_scatter(grad_gate, "dp", scatter_dimension=1, tiled=True),
    )
    shared = lax.psum((summed[2], summed[5], summed[8], summed[9]), "tensor")
    head_sums = lax.psum((grad_dt_shift, grad_log_rate, grad_skip), "dp")
    return (
        block_out,
        grad_hidden,
        summed[0],
        summed[1],
        shared[0],
        summed[3],
        summed[4],
        shared[1],
        summed[6],
        summed[7],
        shared[2],
        shared[3],
        summed[10],
        head_sums[0],
        head_sums[1],
        head_sums[2],
    )


def solution(mesh):
    return jax.shard_map(
        shards,
        mesh=mesh,
        in_specs=(
            P(("dp", "tensor"), None),
            P("dp"),
            P(("dp", "tensor"), None),
            P("dp", "tensor"),
            P("dp", "tensor"),
            P("dp", None),
            P("dp", "tensor"),
            P("tensor", "dp"),
            P("dp"),
            P(None, "tensor", "dp"),
            P("tensor", "dp"),
            P(None, "dp"),
            P("dp"),
            P("tensor", "dp"),
            P("tensor"),
            P("tensor"),
            P("tensor"),
        ),
        out_specs=(
            P(("dp", "tensor"), None),
            P(("dp", "tensor"), None),
            P("dp", "tensor"),
            P("dp", "tensor"),
            P("dp", None),
            P("dp", "tensor"),
            P("tensor", "dp"),
            P("dp"),
            P(None, "tensor", "dp"),
            P("tensor", "dp"),
            P(None, "dp"),
            P("dp"),
            P("tensor", "dp"),
            P("tensor"),
            P("tensor"),
            P("tensor"),
        ),
        check_vma=False,
    )
```

profile of v0, /device:TPU:0, one launch (start us, length us, event | category | flops | bytes accessed | tf_op | source)
XLA Modules:
  0.0 1495.7 jit_solution(4212017841483606342)
XLA Ops:
  8.0 22.3 %all-gather = bf16[8,1,128]{2,1,0:T(2,128)(2,1)S(1)} all-gather(bf16[1,1,128]{2,1,0:T(2,128)(2,1)} %bitcast.791), channel_id=1, replica_groups=mesh['dp'=8,'tensor'=4] {'dp'}, dimensions={0}, use_global_device_ids=true | all-gather | bytes 2304 | tf_op jit(solution)/shard_map/all_gather | solution.py:163
  38.4 32.2 %all_gather.50 = bf16[1024,256]{1,0:T(8,128)(2,1)S(1)} all-gather(bf16[128,256]{1,0:T(8,128)(2,1)S(1)} %copy-done.62), channel_id=1, replica_groups=mesh['dp'=8,'tensor'=4] {'dp'}, dimensions={0}, use_global_device_ids=true | all-gather | bytes 589824 | tf_op jit(solution)/shard_map/all_gather | solution.py:160
  72.2 16.3 %all-gather.1 = bf16[8,32,4]{1,2,0:T(4,128)(2,1)S(1)} all-gather(bf16[1,32,4]{1,2,0:T(4,128)(2,1)S(1)} %bitcast.790), channel_id=1, replica_groups=mesh['dp'=8,'tensor'=4] {'dp'}, dimensions={0}, use_global_device_ids=true | all-gather | bytes 2304 | tf_op jit(solution)/shard_map/all_gather | solution.py:166
  90.2 19.1 %all-reduce.41 = bf16[256]{0:T(256)(128)(2,1)S(1)} all-reduce(bf16[256]{0:T(256)(128)(2,1)S(1)} %dynamic-update-slice), channel_id=1, replica_groups=mesh['dp'=8,'tensor'=4] {'dp'}, use_global_device_ids=true, to_apply=%add.41 | all-reduce | flops 256 | bytes 1024
  109.4 30.6 %all_gather.43 = bf16[4,8,64]{1,0,2:T(4,128)(2,1)S(1)} all-gather(bf16[4,8,8]{1,0,2:T(4,128)(2,1)S(1)} %copy.237), channel_id=1, replica_groups=mesh['dp'=8,'tensor'=4] {'dp'}, dimensions={2}, use_global_device_ids=true | all-gather | bytes 4608 | tf_op jit(solution)/shard_map/all_gather | solution.py:164
  140.8 26.0 %all_gather.42 = bf16[8,64]{0,1:T(8,128)(2,1)S(1)} all-gather(bf16[8,8]{0,1:T(8,128)(2,1)S(1)} %copy.235), channel_id=1, replica_groups=mesh['dp'=8,'tensor'=4] {'dp'}, dimensions={1}, use_global_device_ids=true | all-gather | bytes 1152 | tf_op jit(solution)/shard_map/all_gather | solution.py:165
  166.9 26.2 %all_gather.47 = bf16[1024,8]{0,1:T(8,128)(2,1)S(1)} all-gather(bf16[128,8]{0,1:T(8,128)(2,1)S(1)} %copy-done.86), channel_id=1, replica_groups=mesh['dp'=8,'tensor'=4] {'dp'}, dimensions={0}, use_global_device_ids=true | all-gather | bytes 18432 | tf_op jit(solution)/shard_map/all_gather | solution.py:161
  193.8 26.0 %all_gather.52 = bf16[8,64]{0,1:T(8,128)(2,1)S(1)} all-gather(bf16[8,8]{0,1:T(8,128)(2,1)S(1)} %copy.245), channel_id=1, replica_groups=mesh['dp'=8,'tensor'=4] {'dp'}, dimensions={1}, use_global_device_ids=true | all-gather | bytes 1152 | tf_op jit(solution)/shard_map/all_gather | solution.py:168
  220.5 5.9 fusion.195
  226.4 7.8 fusion.147
  234.2 6.7 copy.243
  240.9 4.8 fusion.196
  245.9 4.5 fusion.163
  256.2 157.7 %while.34 = (s32[]{:T(128)}, f32[3,1024,512]{2,1,0:T(8,128)}, f32[3,1024,512]{1,2,0:T(8,128)}, f32[3,1024,8]{1,2,0:T(8,128)S(1)}, f32[1,8,1]{1,2,0:T(1,128)S(1)}...) while((s32[]{:T(128)}, f32[3,1024,512]{2,1,0:T(8,128)}, ...), condition=%wide.region_4.5_spmd.clone, body=%wide.region_1.4_spmd.clone.sunk | while | flops 3439191552 | bytes 76478392 | solution.py:110
  285.5 10.2 fusion.347
  337.9 10.2 fusion.347
  390.3 10.2 fusion.347
  413.9 14.0 multiply_reduce_fusion.15
  427.9 10.1 psum.63
  438.1 12.2 multiply_reduce_fusion.9
  450.3 10.1 psum.64
  460.4 15.0 %fusion.162 = (f32[3072,512]{1,0:T(8,128)}, bf16[3072,512]{1,0:T(8,128)(2,1)}, bf16[3072,512]{1,0:T(8,128)(2,1)}) fusion(f32[3072]{0:T(1024)S(1)} %psum.64, f32[3072,512]{1,0:T(8,128)} %get-tuple-element.638, f32[3072,512]{1,0:T(8,128)} %get-tuple-element.722, f32[3072]{0:T(1024)S(1)} %get-tuple-element.707, f32[512]{0:T(512)S(1)} %copy-done.83, ...), kind=kLoop, calls=%fused_computation.293 | loop fusion | flops 33030144 | bytes 37787648 | tf_op jit(solution)/shard_map/mul | solution.py:239
  481.6 363.2 %while.35 = (s32[]{:T(128)}, f32[8]{0:T(128)}, f32[8]{0:T(128)}, f32[3,1024,512]{2,1,0:T(8,128)}, f32[3,1024,256]{2,1,0:T(8,128)}, /*index=5*/f32[3,1024,8]{1,2,...) while((s32[]{:T(128)}, f32[8]{0:T(128)}, f32[8]{0:T(128)}, ...), condition=%wide.region_27.28_spmd.clone, body=%wide.region_9.27_spmd.clone.sunk | while | flops 8714870784 | bytes 165069424 | solution.py:110
  509.0 3.9 dynamic-slice_bitcast_fusion.9
  541.7 15.4 %fusion.391 = (f32[4,8,256]{2,1,0:T(8,128)}, f32[4,8,256]{2,1,0:T(8,128)}, f32[4,8,256]{2,1,0:T(8,128)}, f32[4,256,256]{2,1,0:T(8,128)S(1)}) fusion(f32[4,8,256]{2,1,0:T(8,128)S(1)} %copy-done.30, f32[4,256,256]{2,1,0:T(8,128)S(1)} %and_convert_fusion.5, f32[4,256,256]{2,1,0:T(8,128)S(1)} %fusion.389, f32[4,8,256]{2,1,0:T(8,128)S(1)} %bitcast.743, ...), kind=kOutput, calls=%fused_computation.10.clone.1 | convolution fusion | flops 1643356160 | bytes 7503872 | tf_op jit(solution)/shard_map/transpose(jvp())/while/body/eval_jaxpr/checkpoint/chts,cshp->cthp/dot_general | solution.py:42
  564.7 7.5 bitcast_add_fusion.5
  576.1 4.4 add_bitcast_fusion.5
  602.4 9.9 reduce-window.74
  620.0 3.9 dynamic-slice_bitcast_fusion.9
  652.7 15.4 %fusion.391 = (f32[4,8,256]{2,1,0:T(8,128)}, f32[4,8,256]{2,1,0:T(8,128)}, f32[4,8,256]{2,1,0:T(8,128)}, f32[4,256,256]{2,1,0:T(8,128)S(1)}) fusion(f32[4,8,256]{2,1,0:T(8,128)S(1)} %copy-done.30, f32[4,256,256]{2,1,0:T(8,128)S(1)} %and_convert_fusion.5, f32[4,256,256]{2,1,0:T(8,128)S(1)} %fusion.389, f32[4,8,256]{2,1,0:T(8,128)S(1)} %bitcast.743, ...), kind=kOutput, calls=%fused_computation.10.clone.1 | convolution fusion | flops 1643356160 | bytes 7503872 | tf_op jit(solution)/shard_map/transpose(jvp())/while/body/eval_jaxpr/checkpoint/chts,cshp->cthp/dot_general | solution.py:42
  669.2 3.5 fusion.405
  675.7 7.5 bitcast_add_fusion.5
  687.1 4.4 add_bitcast_fusion.5
  713.4 9.9 reduce-window.74
  731.1 3.9 dynamic-slice_bitcast_fusion.9
  763.8 15.4 %fusion.391 = (f32[4,8,256]{2,1,0:T(8,128)}, f32[4,8,256]{2,1,0:T(8,128)}, f32[4,8,256]{2,1,0:T(8,128)}, f32[4,256,256]{2,1,0:T(8,128)S(1)}) fusion(f32[4,8,256]{2,1,0:T(8,128)S(1)} %copy-done.30, f32[4,256,256]{2,1,0:T(8,128)S(1)} %and_convert_fusion.5, f32[4,256,256]{2,1,0:T(8,128)S(1)} %fusion.389, f32[4,8,256]{2,1,0:T(8,128)S(1)} %bitcast.743, ...), kind=kOutput, calls=%fused_computation.10.clone.1 | convolution fusion | flops 1643356160 | bytes 7503872 | tf_op jit(solution)/shard_map/transpose(jvp())/while/body/eval_jaxpr/checkpoint/chts,cshp->cthp/dot_general | solution.py:42
  780.3 3.5 fusion.405
  786.8 7.4 bitcast_add_fusion.5
  798.2 4.4 add_bitcast_fusion.5
  824.4 9.9 reduce-window.74
  844.8 9.3 multiply_reduce_fusion.19
  860.2 15.4 %multiply_reduce_fusion.13 = (f32[512]{0:T(512)S(1)}, f32[512]{0:T(512)S(1)}, f32[512]{0:T(512)S(1)}, f32[512]{0:T(512)S(1)}, f32[512]{0:T(512)S(1)}, /*index=5*/f32[3,1024,512]{2,1,0:T(8,128)S(1)}) fusion(f32[3,1024,512]{2,1,0:T(8,128)} %bitcast.740, f32[3,1024]{1,0:T(4,128)S(1)} %copy-done.43, f32[3,1024]{1,0:T(4,128)S(1)} %copy-done.45, ...), kind=kLoop, calls=%fused_computation.254 | loop fusion | flops 33027584 | bytes 25212928 | tf_op jit(solution)/shard_map/transpose(jvp())/reduce_sum | solution.py:21
  877.5 4.6 fusion.140
  882.1 11.8 reduce-scatter.16.cloned.1.call-done
  897.2 4.8 fusion.198
  902.3 6.8 fusion.197
  909.1 11.1 add_add_fusion
  920.3 4.4 fusion.170
  924.8 7.6 fusion.200
  932.4 8.6 fusion.199
  941.1 7.5 fusion.201
  951.8 4.9 all-to-all-start
  959.9 57.0 %all-gather.17.cloned.1.call-done = bf16[2048,1024]{1,0:T(8,128)(2,1)} async-done(((bf16[512,1024]{1,0:T(8,128)(2,1)}), bf16[2048,1024]{1,0:T(8,128)(2,1)}) %all-gather.17.cloned.1.call-update) | async-done | bytes 4194320 | tf_op jit(solution)/shard_map/all_gather | solution.py:229
  1016.9 7.8 fusion.156
  1024.6 59.5 %reduce-scatter.22.cloned.1.call-done = f32[128,256]{1,0:T(8,128)} async-done(((f32[1024,256]{1,0:T(8,128)}), f32[128,256]{1,0:T(8,128)}) %reduce-scatter.22.cloned.1.call-update) | async-done | bytes 131088 | tf_op jit(solution)/shard_map/reduce_scatter | solution.py:281
  1084.2 100.5 %reduce-scatter.14.cloned.1.call-done = f32[768,1024]{1,0:T(8,128)} async-done(((f32[3072,1024]{1,0:T(8,128)}), f32[768,1024]{1,0:T(8,128)}) %reduce-scatter.14.cloned.1.call-update) | async-done | bytes 3145744 | tf_op jit(solution)/shard_map/reduce_scatter | solution.py:262
  1184.7 5.1 fusion.161
  1189.8 37.1 %all-reduce.47 = (f32[1024]{0:T(1024)S(1)}, f32[4,8,64]{2,1,0:T(8,128)S(1)}, f32[8,64]{1,0:T(8,128)S(1)}, f32[256]{0:T(256)S(1)}, f32[8,64]{1,0:T(8,128)S(1)}, /*index=5*/f32[8]{0:T(128)}, f32[8]{0:T(128)}, f32[8]{0:T(128)}) all-reduce(f32[1024]{0:T(1024)S(1)} %get-tuple-element.571, ...), channel_id=9, replica_groups=mesh['dp'=8,'tensor'=4] {'dp'}, use_global_device_ids=true, to_apply=%region_38.39.clone | all-reduce | flops 4376 | bytes 35008
  1227.7 6.5 all-reduce.48
  1234.2 4.4 fusion.158
  1241.9 70.9 %reduce-scatter.20.cloned.1.call-done = f32[128,512]{1,0:T(8,128)} async-done(((f32[1024,512]{1,0:T(8,128)}), f32[128,512]{1,0:T(8,128)}) %reduce-scatter.20.cloned.1.call-update) | async-done | bytes 262160 | tf_op jit(solution)/shard_map/reduce_scatter | solution.py:280
  1312.8 70.7 %reduce-scatter.18.cloned.1.call-done = f32[128,512]{1,0:T(8,128)} async-done(((f32[1024,512]{1,0:T(8,128)}), f32[128,512]{1,0:T(8,128)}) %reduce-scatter.18.cloned.1.call-update) | async-done | bytes 262160 | tf_op jit(solution)/shard_map/reduce_scatter | solution.py:279
  1383.5 71.1 %reduce-scatter.26.cloned.1.call-done = f32[512,128]{1,0:T(8,128)} async-done(((f32[512,1024]{1,0:T(8,128)}), f32[512,128]{1,0:T(8,128)}) %reduce-scatter.26.cloned.1.call-update) | async-done | bytes 262160 | tf_op jit(solution)/shard_map/reduce_scatter | solution.py:283
  1454.6 32.6 %all-reduce.51.cloned.1.call-done = f32[128,256]{1,0:T(8,128)} async-done(((f32[128,256]{1,0:T(8,128)}), f32[128,256]{1,0:T(8,128)}) %all-reduce.51.cloned.1.call-update) | async-done | bytes 131088 | tf_op jit(solution)/shard_map/psum | solution.py:291
  (796 shorter events, 358.5 us)
Async XLA Ops:
  7.2 213.3 %all-gather.11.cloned.1.call-start = ((), (), s32[]{:S(2)}) async-start(), calls=%async_computation.10 | async-start | bytes 1179648 | tf_op jit(solution)/shard_map/all_gather | solution.py:159
  7.9 212.6 %all-gather.9.cloned.1.call-start = ((), (), s32[]{:S(2)}) async-start(), calls=%async_computation.9 | async-start | bytes 7864320 | tf_op jit(solution)/shard_map/all_gather | solution.py:173
  33.3 37.3 %copy-start.74 = (s32[3072]{0:T(1024)S(1)}, s32[3072]{0:T(1024)}, u32[]{:S(2)}) copy-start(s32[3072]{0:T(1024)} %param.22) | copy-start | bytes 36868
  33.3 39.0 %copy-start.91 = (bf16[4,32]{1,0:T(4,128)(2,1)S(1)}, bf16[4,32]{1,0:T(4,128)(2,1)}, u32[]{:S(2)}) copy-start(bf16[4,32]{1,0:T(4,128)(2,1)} %param.32) | copy-start | bytes 772
  33.3 55.4 %copy-start.88 = (u32[32]{0:T(128)S(1)}, u32[32]{0:T(128)}, u32[]{:S(2)}) copy-start(u32[32]{0:T(128)} %constant.207) | copy-start | bytes 388
  33.3 56.7 %copy-start.93 = (bf16[32]{0:T(256)(128)(2,1)S(1)}, bf16[32]{0:T(256)(128)(2,1)}, u32[]{:S(2)}) copy-start(bf16[32]{0:T(256)(128)(2,1)} %param.33) | copy-start | bytes 196
  33.3 76.0 %copy-start.84 = (bf16[4,8,8]{2,1,0:T(8,128)(2,1)S(1)}, bf16[4,8,8]{2,1,0:T(8,128)(2,1)}, u32[]{:S(2)}) copy-start(bf16[4,8,8]{2,1,0:T(8,128)(2,1)} %param.30) | copy-start | bytes 1540
  36.3 104.3 %copy-start.89 = (bf16[8,8]{1,0:T(8,128)(2,1)S(1)}, bf16[8,8]{1,0:T(8,128)(2,1)}, u32[]{:S(2)}) copy-start(bf16[8,8]{1,0:T(8,128)(2,1)} %param.31) | copy-start | bytes 388
  36.3 130.6 %copy-start.86 = (bf16[128,8]{0,1:T(8,128)(2,1)S(1)}, bf16[128,8]{0,1:T(8,128)(2,1)}, u32[]{:S(2)}) copy-start(bf16[128,8]{0,1:T(8,128)(2,1)} %param.27) | copy-start | bytes 6148
  36.3 156.8 %copy-start.94 = (f32[8]{0:T(128)S(1)}, f32[8]{0:T(128)}, u32[]{:S(2)}) copy-start(f32[8]{0:T(128)} %param.36) | copy-start | bytes 100
  36.3 157.3 %copy-start.90 = (bf16[8,8]{1,0:T(8,128)(2,1)S(1)}, bf16[8,8]{1,0:T(8,128)(2,1)}, u32[]{:S(2)}) copy-start(bf16[8,8]{1,0:T(8,128)(2,1)} %param.34) | copy-start | bytes 388
  36.4 377.5 %all-gather.13.cloned.1.call-start = ((), (), s32[]{:S(2)}) async-start(), calls=%async_computation.11 | async-start | bytes 1179648 | tf_op jit(solution)/shard_map/all_gather | solution.py:158
  37.1 400.9 %all-gather.15.cloned.1.call-start = ((), (), s32[]{:S(2)}) async-start(), calls=%async_computation.12 | async-start | bytes 1179648 | tf_op jit(solution)/shard_map/all_gather | solution.py:162
  37.7 400.4 %all-gather.19.cloned.1.call-start = ((), (), s32[]{:S(2)}) async-start(), calls=%async_computation.14 | async-start | bytes 7864320 | tf_op jit(solution)/shard_map/all_gather | solution.py:233
  38.3 855.6 %reduce-scatter.16.cloned.1.call-start = ((), (), s32[]{:S(2)}) async-start(), calls=%async_computation.16 | async-start | bytes 3932160 | tf_op jit(solution)/shard_map/reduce_scatter | solution.py:263
  70.5 170.4 %copy-start.34 = (bf16[1024,256]{1,0:T(8,128)(2,1)}, bf16[1024,256]{1,0:T(8,128)(2,1)S(1)}, u32[]{:S(2)}) copy-start(bf16[1024,256]{1,0:T(8,128)(2,1)S(1)} %all_gather.50) | copy-start | bytes 1572868
  72.2 173.6 %copy-start.40 = (f32[3,1024]{1,0:T(4,128)}, f32[3,1024]{1,0:T(4,128)S(1)}, u32[]{:S(2)}) copy-start(f32[3,1024]{1,0:T(4,128)S(1)} %get-tuple-element.704) | copy-start | bytes 36868
  72.2 173.6 %copy-start.42 = (f32[3,1024]{1,0:T(4,128)}, f32[3,1024]{1,0:T(4,128)S(1)}, u32[]{:S(2)}) copy-start(f32[3,1024]{1,0:T(4,128)S(1)} %get-tuple-element.705) | copy-start | bytes 36868
  72.2 173.6 %copy-start.44 = (f32[3,1024]{1,0:T(4,128)}, f32[3,1024]{1,0:T(4,128)S(1)}, u32[]{:S(2)}) copy-start(f32[3,1024]{1,0:T(4,128)S(1)} %get-tuple-element.706) | copy-start | bytes 36868
  88.7 157.2 %copy-start.75 = (f32[1,256]{1,0:T(1,128)}, f32[1,256]{1,0:T(1,128)S(1)}, u32[]{:S(2)}) copy-start(f32[1,256]{1,0:T(1,128)S(1)} %get-tuple-element.711) | copy-start | bytes 3076
  88.7 157.2 %copy-start.77 = (f32[1,256]{1,0:T(1,128)}, f32[1,256]{1,0:T(1,128)S(1)}, u32[]{:S(2)}) copy-start(f32[1,256]{1,0:T(1,128)S(1)} %get-tuple-element.712) | copy-start | bytes 3076
  88.7 157.2 %copy-start.79 = (f32[1,256]{1,0:T(1,128)}, f32[1,256]{1,0:T(1,128)S(1)}, u32[]{:S(2)}) copy-start(f32[1,256]{1,0:T(1,128)S(1)} %get-tuple-element.713) | copy-start | bytes 3076
  88.7 157.2 %copy-start.81 = (f32[1,256]{1,0:T(1,128)}, f32[1,256]{1,0:T(1,128)S(1)}, u32[]{:S(2)}) copy-start(f32[1,256]{1,0:T(1,128)S(1)} %get-tuple-element.714) | copy-start | bytes 3076
  140.2 86.2 %copy-start.64 = (f32[512]{0:T(512)}, f32[512]{0:T(512)S(1)}, u32[]{:S(2)}) copy-start(f32[512]{0:T(512)S(1)} %mul.1375) | copy-start | bytes 6148
  140.4 86.0 %copy-start.66 = (f32[512]{0:T(512)}, f32[512]{0:T(512)S(1)}, u32[]{:S(2)}) copy-start(f32[512]{0:T(512)S(1)} %mul.1383) | copy-start | bytes 6148
  140.5 85.9 %copy-start.68 = (f32[512]{0:T(512)}, f32[512]{0:T(512)S(1)}, u32[]{:S(2)}) copy-start(f32[512]{0:T(512)S(1)} %mul.1388) | copy-start | bytes 6148
  140.7 85.8 %copy-start.70 = (f32[512]{0:T(512)}, f32[512]{0:T(512)S(1)}, u32[]{:S(2)}) copy-start(f32[512]{0:T(512)S(1)} %mul.1393) | copy-start | bytes 6148
  193.2 57.2 %copy-start.56 = (bf16[1024,8]{0,1:T(8,128)(2,1)}, bf16[1024,8]{0,1:T(8,128)(2,1)S(1)}, u32[]{:S(2)}) copy-start(bf16[1024,8]{0,1:T(8,128)(2,1)S(1)} %all_gather.47) | copy-start | bytes 49156
  234.2 16.1 %slice-start.1 = ((s8[6291456]{0:T(1024)(128)(4,1)}), s8[2097152]{0:T(1024)(128)(4,1)S(1)}, s32[]{:S(2)}) async-start(s8[6291456]{0:T(1024)(128)(4,1)} %bitcast.733), calls=%async_computation.25 | async-start | bytes 4194304
  413.9 24.2 %copy-start.83 = (f32[512]{0:T(512)S(1)}, f32[512]{0:T(512)}, u32[]{:S(2)}) copy-start(f32[512]{0:T(512)} %reshape.822) | copy-start | bytes 6148
  509.0 14.8 copy-start
  525.9 32.2 %copy-start.5 = (f32[8,64,128]{2,1,0:T(8,128)}, f32[8,64,128]{2,1,0:T(8,128)S(1)}, u32[]{:S(2)}) copy-start(f32[8,64,128]{2,1,0:T(8,128)S(1)} %fusion.392) | copy-start | bytes 786436 | tf_op jit(solution)/shard_map/transpose(jvp())/while
  596.0 16.4 %copy-start.37 = (f32[4,8,256]{2,1,0:T(8,128)S(1)}, f32[4,8,256]{2,1,0:T(8,128)}, u32[]{:S(2)}) copy-start(f32[4,8,256]{2,1,0:T(8,128)} %get-tuple-element.968) | copy-start | bytes 98308 | tf_op jit(solution)/shard_map/transpose(jvp())/while
  597.5 17.5 %copy-start.36 = (f32[3,1024,8]{1,2,0:T(8,128)S(1)}, f32[3,1024,8]{1,2,0:T(8,128)}, u32[]{:S(2)}) copy-start(f32[3,1024,8]{1,2,0:T(8,128)} %copy-done.35) | copy-start | bytes 294916 | tf_op jit(solution)/shard_map/transpose(jvp())/while
  620.0 14.8 copy-start
  625.2 13.7 copy-start.2
  637.0 32.2 %copy-start.5 = (f32[8,64,128]{2,1,0:T(8,128)}, f32[8,64,128]{2,1,0:T(8,128)S(1)}, u32[]{:S(2)}) copy-start(f32[8,64,128]{2,1,0:T(8,128)S(1)} %fusion.392) | copy-start | bytes 786436 | tf_op jit(solution)/shard_map/transpose(jvp())/while
  707.0 16.4 %copy-start.37 = (f32[4,8,256]{2,1,0:T(8,128)S(1)}, f32[4,8,256]{2,1,0:T(8,128)}, u32[]{:S(2)}) copy-start(f32[4,8,256]{2,1,0:T(8,128)} %get-tuple-element.968) | copy-start | bytes 98308 | tf_op jit(solution)/shard_map/transpose(jvp())/while
  708.5 17.6 %copy-start.36 = (f32[3,1024,8]{1,2,0:T(8,128)S(1)}, f32[3,1024,8]{1,2,0:T(8,128)}, u32[]{:S(2)}) copy-start(f32[3,1024,8]{1,2,0:T(8,128)} %copy-done.35) | copy-start | bytes 294916 | tf_op jit(solution)/shard_map/transpose(jvp())/while
  731.1 14.8 copy-start
  736.3 13.7 copy-start.2
  748.1 32.2 %copy-start.5 = (f32[8,64,128]{2,1,0:T(8,128)}, f32[8,64,128]{2,1,0:T(8,128)S(1)}, u32[]{:S(2)}) copy-start(f32[8,64,128]{2,1,0:T(8,128)S(1)} %fusion.392) | copy-start | bytes 786436 | tf_op jit(solution)/shard_map/transpose(jvp())/while
  818.1 16.4 %copy-start.37 = (f32[4,8,256]{2,1,0:T(8,128)S(1)}, f32[4,8,256]{2,1,0:T(8,128)}, u32[]{:S(2)}) copy-start(f32[4,8,256]{2,1,0:T(8,128)} %get-tuple-element.968) | copy-start | bytes 98308 | tf_op jit(solution)/shard_map/transpose(jvp())/while
  819.6 17.5 %copy-start.36 = (f32[3,1024,8]{1,2,0:T(8,128)S(1)}, f32[3,1024,8]{1,2,0:T(8,128)}, u32[]{:S(2)}) copy-start(f32[3,1024,8]{1,2,0:T(8,128)} %copy-done.35) | copy-start | bytes 294916 | tf_op jit(solution)/shard_map/transpose(jvp())/while
  858.5 100.6 %reduce-scatter.28.cloned.1.call-start = ((), (), s32[]{:S(2)}) async-start(), calls=%async_computation.23 | async-start | bytes 147456
  859.4 157.5 %all-gather.17.cloned.1.call-start = ((), (), s32[]{:S(2)}) async-start(), calls=%async_computation.13 | async-start | bytes 5242880 | tf_op jit(solution)/shard_map/all_gather | solution.py:229
  860.1 224.0 %reduce-scatter.22.cloned.1.call-start = ((), (), s32[]{:S(2)}) async-start(), calls=%async_computation.19 | async-start | bytes 1179648 | tf_op jit(solution)/shard_map/reduce_scatter | solution.py:281
  860.2 15.4 %copy-start.67 = (f32[512]{0:T(512)S(1)}, f32[512]{0:T(512)}, u32[]{:S(2)}) copy-start(f32[512]{0:T(512)} %copy-done.66) | copy-start | bytes 6148
  860.2 15.4 %copy-start.69 = (f32[512]{0:T(512)S(1)}, f32[512]{0:T(512)}, u32[]{:S(2)}) copy-start(f32[512]{0:T(512)} %copy-done.68) | copy-start | bytes 6148
  860.2 15.4 %copy-start.71 = (f32[512]{0:T(512)S(1)}, f32[512]{0:T(512)}, u32[]{:S(2)}) copy-start(f32[512]{0:T(512)} %copy-done.70) | copy-start | bytes 6148
  882.1 15.1 %copy-start.33 = (bf16[3,1024,512]{2,1,0:T(8,128)(2,1)S(1)}, bf16[3,1024,512]{2,1,0:T(8,128)(2,1)}, u32[]{:S(2)}) copy-start(bf16[3,1024,512]{2,1,0:T(8,128)(2,1)} %fusion.140) | copy-start | bytes 9437188
  897.1 287.6 %reduce-scatter.14.cloned.1.call-start = ((), (), s32[]{:S(2)}) async-start(), calls=%async_computation.15 | async-start | bytes 15728640 | tf_op jit(solution)/shard_map/reduce_scatter | solution.py:262
  920.3 321.6 %reduce-scatter.24.cloned.1.call-start = ((), (), s32[]{:S(2)}) async-start(), calls=%async_computation.21 | async-start | bytes 36864 | tf_op jit(solution)/shard_map/reduce_scatter | solution.py:282
  924.7 388.1 %reduce-scatter.20.cloned.1.call-start = ((), (), s32[]{:S(2)}) async-start(), calls=%async_computation.18 | async-start | bytes 2359296 | tf_op jit(solution)/shard_map/reduce_scatter | solution.py:280
  932.4 451.2 %reduce-scatter.18.cloned.1.call-start = ((), (), s32[]{:S(2)}) async-start(), calls=%async_computation.17 | async-start | bytes 2359296 | tf_op jit(solution)/shard_map/reduce_scatter | solution.py:279
  941.1 513.5 %reduce-scatter.26.cloned.1.call-start = ((), (), s32[]{:S(2)}) async-start(), calls=%async_computation.22 | async-start | bytes 2359296 | tf_op jit(solution)/shard_map/reduce_scatter | solution.py:283
  951.7 65.1 %copy-start.23 = (bf16[768,1024]{1,0:T(8,128)(2,1)S(1)}, bf16[768,1024]{1,0:T(8,128)(2,1)}, u32[]{:S(2)}) copy-start(bf16[768,1024]{1,0:T(8,128)(2,1)} %param.21) | copy-start | bytes 4718596
  951.8 65.1 %all-to-all-start = ((bf16[4,768,512]{1,2,0:T(8,128)(2,1)}), bf16[4,768,512]{1,2,0:T(8,128)(2,1)}, u32[]{:S(2)}, u32[]{:S(2)}) async-start(bf16[4,768,512]{1,2,0:T(8,128)(2,1)} %copy.247), calls=%async_computation | async-start | bytes 6291456 | tf_op jit(solution)/shard_map/all_to_all | solution.py:228
  956.6 530.6 %all-reduce.51.cloned.1.call-start = ((), (), s32[]{:S(2)}) async-start(), calls=%async_computation.20 | async-start | bytes 262144 | tf_op jit(solution)/shard_map/psum | solution.py:291
  1016.9 167.9 %copy-start.59 = (f32[768]{0:T(1024)S(1)}, f32[768]{0:T(1024)}, u32[]{:S(2)}) copy-start(f32[768]{0:T(1024)} %copy-done.58) | copy-start | bytes 9220
  1016.9 167.9 %copy-start.61 = (f32[8,1,128]{2,1,0:T(1,128)S(1)}, f32[8,1,128]{2,1,0:T(1,128)}, u32[]{:S(2)}) copy-start(f32[8,1,128]{2,1,0:T(1,128)} %copy-done.60) | copy-start | bytes 12292
  1084.2 105.6 %copy-start.63 = (f32[8]{0:T(128)S(1)}, f32[8]{0:T(128)}, u32[]{:S(2)}) copy-start(f32[8]{0:T(128)} %get-tuple-element.334) | copy-start | bytes 100
  1084.2 150.0 %copy-start.28 = (bf16[768,1024]{1,0:T(8,128)(2,1)S(1)}, bf16[768,1024]{1,0:T(8,128)(2,1)}, u32[]{:S(2)}) copy-start(bf16[768,1024]{1,0:T(8,128)(2,1)} %param.23) | copy-start | bytes 4718596
  1084.2 150.0 %copy-start.72 = (f32[768]{0:T(1024)S(1)}, f32[768]{0:T(1024)}, u32[]{:S(2)}) copy-start(f32[768]{0:T(1024)} %get-tuple-element.709) | copy-start | bytes 9220
  (133 other events, 697.9 us)
Sparse Core Ops, SparseCore 0:
  10.1 45.6 all-gather.10
  58.0 45.5 all-gather.8
  105.7 40.2 all-gather.12
  147.9 38.3 all-gather.14
  187.8 45.7 all-gather.18
  858.6 35.2 reduce-scatter.15
  898.1 60.9 reduce-scatter.27
  960.7 56.0 all-gather.16
  1020.7 63.4 reduce-scatter.21
  1086.6 98.0 reduce-scatter.13
  1188.4 53.4 reduce-scatter.23
  1245.9 66.9 reduce-scatter.19
  1316.9 66.5 reduce-scatter.17
  1387.5 67.0 reduce-scatter.25
  1456.8 30.3 all-reduce.50
where the time goes:
time: 1510 us; the launch traced here: 1500 us
  waiting for transfers between devices  480 us (32%)
  matrix products  300 us (20%)
  blocking collectives  262 us (17%)
  other arithmetic  205 us (14%)
  local copies, waits for them, and re-layouts  176 us (12%)
  loops' own time  48.6 us (3%)
  between operations  17.8 us (1%)
    reduce_scatter x1, waiting for transfers between devices, shards(): lax.psum_scatter(d_normed_part, 'tensor', scatter_dimension=0, tiled=True)  101 us
    dot_general x9, matrix products, scan_sequence(): jnp.einsum('chts,cshp->cthp', weights, value_blocks, precision=HIGHEST)  99.2 us
    reduce_scatter x1, waiting for transfers between devices, shards(): lax.psum_scatter(grad_out, 'dp', scatter_dimension=1, tiled=True)  71.1 us
    reduce_scatter x1, waiting for transfers between devices, shards(): lax.psum_scatter(grad_x, 'dp', scatter_dimension=0, tiled=True)  70.9 us
    reduce_scatter x1, waiting for transfers between devices, shards(): lax.psum_scatter(grad_z, 'dp', scatter_dimension=0, tiled=True)  70.7 us
    reduce_scatter x1, waiting for transfers between devices, shards(): lax.psum_scatter(grad_bc_part, 'dp', scatter_dimension=0, tiled=True)  59.5 us
    all_gather x1, waiting for transfers between devices, shards(): out_full = lax.all_gather(proj_out, 'tensor', axis=0, tiled=True)  57 us
    unnamed x2, blocking collectives  56.2 us
  transfers between devices with their start and end apart: 16, of which 10 were waited for; matrix products, arithmetic and copies ran while one was open for 21% of the time, Pallas kernels for 0%

commit v1 on v0

v1 whole, which is shorter than its diff:
```python
import functools

import jax
import jax.numpy as jnp
from jax import lax
from jax.experimental import pallas as pl
from jax.experimental.pallas import tpu as pltpu
from jax.sharding import PartitionSpec as P

SEQ_LEN = 1024
EPSILON = 1e-05
T = 128
F32 = jnp.float32
BF16 = jnp.bfloat16


def mm(a, b):
    return lax.dot_general(a, b, (((1,), (0,)), ((), ())), preferred_element_type=F32)


def mm_nt(a, b):
    return lax.dot_general(a, b, (((1,), (1,)), ((), ())), preferred_element_type=F32)


def mm_tn(a, b):
    return lax.dot_general(a, b, (((0,), (0,)), ((), ())), preferred_element_type=F32)


def split2(v):
    hi = v.astype(BF16)
    return hi, (v - hi.astype(F32)).astype(BF16)


def split3(v):
    hi = v.astype(BF16)
    rest = v - hi.astype(F32)
    mid = rest.astype(BF16)
    return hi, mid, (rest - mid.astype(F32)).astype(BF16)


def sigmoid(v):
    return 1.0 / (1.0 + jnp.exp(-v))


def softplus(v):
    return jnp.maximum(v, 0.0) + jnp.log(1.0 + jnp.exp(-jnp.abs(v)))


def expand(v, spread):
    hi, lo = split2(v)
    return mm(hi, spread) + mm(lo, spread)


def per_head(v, spread):
    hi, lo = split2(v)
    return mm_nt(hi, spread) + mm_nt(lo, spread)


def decay_parts(dt_raw, dt_bias, rate, aux, spread):
    steps = softplus(dt_raw + dt_bias)
    rows = lax.broadcasted_iota(jnp.int32, (T, T), 0)
    cols = lax.broadcasted_iota(jnp.int32, (T, T), 1)
    tri = (rows >= cols).astype(BF16)
    p0, p1, p2 = split3(steps * rate)
    cum = mm(tri, p0) + mm(tri, p1) + mm(tri, p2)
    reach, tail = aux[:, 1:2], aux[:, 2:3]
    entry = jnp.exp(cum) * reach
    to_end = jnp.exp(cum[T - 1 : T] - cum) * tail
    wide = expand(jnp.concatenate([steps, entry, to_end], 0), spread)
    return steps, cum, tri, wide[:T], wide[T : 2 * T], wide[2 * T :], rows >= cols


def decay_of(cum, cum_t, mask, h):
    return jnp.exp(jnp.where(mask, cum[:, h : h + 1] - cum_t[h : h + 1, :], -1e30))


def halves(v):
    low = lax.broadcasted_iota(jnp.int32, v.shape, 1) < v.shape[1] // 2
    zero = jnp.zeros_like(v)
    return jnp.where(low, v, zero), jnp.where(low, zero, v)


def forward_kernel(
    heads, di, ns,
    proj_ref, dyn_ref, aux_ref, seg_ref, filt_ref, bias_ref, head_ref, chan_ref, spread_ref,
    pre_ref, y_ref, v_ref, state_out_ref, stats_ref,
    ext, state,
):
    @pl.when(pl.program_id(0) == 0)
    def _():
        ext[...] = jnp.zeros_like(ext)
        state[...] = jnp.zeros_like(state)

    aux = aux_ref[...]
    spread = spread_ref[...]
    raw = proj_ref[:, di : 2 * di + 2 * ns]
    ext[8:, :] = raw
    filt = filt_ref[...]
    pre = bias_ref[...] + filt[3:4] * raw
    for k in range(1, 4):
        pre = pre + filt[3 - k : 4 - k] * (ext[8 - k : 8 - k + T, :] * aux[:, 2 + k : 3 + k])
    ext[0:8, :] = ext[T : T + 8, :]
    pre_ref[...] = pre
    act = pre * sigmoid(pre)
    xc = act[:, :di]
    b_low = act[:, di : di + ns].astype(BF16)
    c_low = act[:, di + ns :].astype(BF16)
    dt_raw = proj_ref[:, 2 * di + 2 * ns :]
    steps, cum, tri, dt_e, entry_e, end_e, causal = decay_parts(
        dt_raw, head_ref[0:1], head_ref[1:2], aux, spread
    )
    cum_t = cum.T
    mask = causal & (aux[:, 0:1] == seg_ref[0])
    xdt = xc * dt_e
    xdt_low = xdt.astype(BF16)
    scores = mm_nt(c_low, b_low)
    pieces = []
    for j in range(heads // 2):
        pair = xdt_low[:, 128 * j : 128 * (j + 1)]
        xa, xb = halves(pair)
        ma = (decay_of(cum, cum_t, mask, 2 * j) * scores).astype(BF16)
        mb = (decay_of(cum, cum_t, mask, 2 * j + 1) * scores).astype(BF16)
        pieces.append(mm(jnp.concatenate([ma, mb], 1), jnp.concatenate([xa, xb], 0)))
    state_low = state[...].astype(BF16)
    state_out_ref[0] = state_low
    chan = chan_ref[...]
    y = (
        jnp.concatenate(pieces, 1)
        + entry_e * mm(c_low, state_low)
        + chan[0:1] * xc
    )
    state[...] = entry_e[T - 1 : T] * state[...] + mm_tn(b_low, (end_e * xdt).astype(BF16))
    y_ref[...] = y
    z = proj_ref[:, :di]
    u = y * z * sigmoid(z)
    v = u * chan[1:2]
    v_ref[...] = v.astype(BF16)
    ones = jnp.ones((8, di), BF16)
    s_hi, s_lo = split2(u * u)
    i_hi, i_lo = split2(v * dyn_ref[...])
    square = mm_nt(ones, s_hi) + mm_nt(ones, s_lo)
    inner = mm_nt(ones, i_hi) + mm_nt(ones, i_lo)
    upper = lax.broadcasted_iota(jnp.int32, (8, T), 0) < 4
    stats_ref[0] = jnp.where(upper, square, inner)


def backward_kernel(
    heads, di, ns,
    proj_ref, dyn_ref, pre_ref, y_ref, state_ref, aux_ref, aux2_ref, seg_ref,
    filt_ref, head_ref, chan_ref, spread_ref,
    d_ref, conv_acc, chan_acc, head_acc,
    ext, d_state,
):
    @pl.when(pl.program_id(0) == 0)
    def _():
        ext[...] = jnp.zeros_like(ext)
        d_state[...] = jnp.zeros_like(d_state)
        conv_acc[...] = jnp.zeros_like(conv_acc)
        chan_acc[...] = jnp.zeros_like(chan_acc)
        head_acc[...] = jnp.zeros_like(head_acc)

    aux = aux_ref[...]
    spread = spread_ref[...]
    chan = chan_ref[...]
    skip, gain = chan[0:1], chan[1:2]
    inv, slope = aux2_ref[:, 0:1], aux2_ref[:, 1:2]
    y = y_ref[...]
    dyn = dyn_ref[...]
    z = proj_ref[:, :di]
    sig_z = sigmoid(z)
    silu_z = z * sig_z
    u = y * silu_z
    d_u = inv * gain * dyn - u * slope
    d_ref[:, :di] = (d_u * y * sig_z * (1.0 + z * (1.0 - sig_z))).astype(BF16)
    chan_acc[0:1, :] += jnp.sum(dyn * u * inv, 0, keepdims=True)
    dy = d_u * silu_z
    dy_low = dy.astype(BF16)
    dy_r = dy_low.astype(F32)

    pre = pre_ref[...]
    sig = sigmoid(pre)
    act = pre * sig
    d_act = sig * (1.0 + pre * (1.0 - sig))
    xc = act[:, :di]
    b_low = act[:, di : di + ns].astype(BF16)
    c_low = act[:, di + ns :].astype(BF16)
    rate = head_ref[1:2]
    dt_in = proj_ref[:, 2 * di + 2 * ns :] + head_ref[0:1]
    steps, cum, tri, dt_e, entry_e, end_e, causal = decay_parts(
        proj_ref[:, 2 * di + 2 * ns :], head_ref[0:1], rate, aux, spread
    )
    cum_t = cum.T
    mask = causal & (aux[:, 0:1] == seg_ref[0])
    xdt = xc * dt_e
    xdt_low = xdt.astype(BF16)
    xend_low = (end_e * xdt).astype(BF16)
    scores = mm_nt(c_low, b_low)
    d_scores = jnp.zeros((T, T), F32)
    pieces = []
    for j in range(heads // 2):
        lanes = slice(128 * j, 128 * (j + 1))
        xa, xb = halves(xdt_low[:, lanes])
        dya, dyb = halves(dy_low[:, lanes])
        la = decay_of(cum, cum_t, mask, 2 * j)
        lb = decay_of(cum, cum_t, mask, 2 * j + 1)
        ma = (la * scores).astype(BF16)
        mb = (lb * scores).astype(BF16)
        dm = mm_nt(dy_low[:, lanes], jnp.concatenate([xa, xb], 0))
        d_scores = d_scores + la * dm[:, :T] + lb * dm[:, T:]
        pieces.append(mm_tn(jnp.concatenate([ma, mb], 0), jnp.concatenate([dya, dyb], 0)))
    dx_intra = jnp.concatenate(pieces, 1)
    s_in = state_ref[0]
    ds_low = d_state[...].astype(BF16)
    dx_end = mm(b_low, ds_low)
    ey_low = (entry_e * dy_r).astype(BF16)
    ds_scores = d_scores.astype(BF16)
    d_c = mm(ds_scores, b_low) + mm_nt(ey_low, s_in)
    d_b = mm_tn(ds_scores, c_low) + mm_nt(xend_low, ds_low)
    d_xdt = dx_intra + end_e * dx_end
    d_xc = dt_e * d_xdt + skip * dy
    chan_acc[1:2, :] += jnp.sum(dy * xc, 0, keepdims=True)
    ended = xend_low.astype(F32) * dx_end
    keep_e = entry_e[T - 1 : T]
    total = jnp.sum(ended, 0, keepdims=True) + keep_e * jnp.sum(
        d_state[...] * s_in.astype(F32), 0, keepdims=True
    )
    last = lax.broadcasted_iota(jnp.int32, (T, 1), 0) == T - 1
    flow = dy_r * (y - skip * xc) - xdt_low.astype(F32) * dx_intra - ended
    flow = flow + jnp.where(last, total, 0.0)
    d_state[...] = keep_e * d_state[...] + mm_tn(c_low, ey_low)
    sums = per_head(jnp.concatenate([flow, d_xdt * xc], 0), spread)
    q0, q1, q2 = split3(sums[:T])
    d_log = mm_tn(tri, q0) + mm_tn(tri, q1) + mm_tn(tri, q2)
    d_dt = (sums[T:] + rate * d_log) * sigmoid(dt_in)
    d_ref[:, 2 * di + 2 * ns :] = d_dt.astype(BF16)
    head_acc[0:1, :] += jnp.sum(d_dt, 0, keepdims=True)
    head_acc[1:2, :] += jnp.sum(d_log * steps, 0, keepdims=True)

    d_pre = jnp.concatenate([d_xc, d_b, d_c], 1) * d_act
    ext[0:T, :] = d_pre
    raw = proj_ref[:, di : 2 * di + 2 * ns]
    filt = filt_ref[...]
    d_raw = filt[3:4] * d_pre
    conv_acc[3:4, :] += jnp.sum(raw * d_pre, 0, keepdims=True)
    conv_acc[4:5, :] += jnp.sum(d_pre, 0, keepdims=True)
    for k in range(1, 4):
        moved = ext[k : k + T, :] * aux[:, 5 + k : 6 + k]
        d_raw = d_raw + filt[3 - k : 4 - k] * moved
        conv_acc[3 - k : 4 - k, :] += jnp.sum(raw * moved, 0, keepdims=True)
    ext[T : T + 8, :] = ext[0:8, :]
    d_ref[:, di : 2 * di + 2 * ns] = d_raw.astype(BF16)


def whole(shape):
    return pl.BlockSpec(shape, lambda i: (0,) * len(shape))


def run_forward(heads, di, ns, proj, dyn, aux, seg_rows, filt, bias, head, chan, spread):
    tokens, width = proj.shape
    count = tokens // T
    conv = di + 2 * ns
    row = lambda w: pl.BlockSpec((T, w), lambda i: (i, 0))
    return pl.pallas_call(
        functools.partial(forward_kernel, heads, di, ns),
        grid=(count,),
        in_specs=[
            row(width), row(di), row(16),
            pl.BlockSpec((1, 1, T), lambda i: (i, 0, 0)),
            whole(filt.shape), whole(bias.shape), whole(head.shape),
            whole(chan.shape), whole(spread.shape),
        ],
        out_specs=[
            row(conv), row(di), row(di),
            pl.BlockSpec((1, ns, di), lambda i: (i, 0, 0)),
            pl.BlockSpec((1, 8, T), lambda i: (i, 0, 0)),
        ],
        out_shape=[
            jax.ShapeDtypeStruct((tokens, conv), F32),
            jax.ShapeDtypeStruct((tokens, di), F32),
            jax.ShapeDtypeStruct((tokens, di), BF16),
            jax.ShapeDtypeStruct((count, ns, di), BF16),
            jax.ShapeDtypeStruct((count, 8, T), F32),
        ],
        scratch_shapes=[pltpu.VMEM((T + 8, conv), F32), pltpu.VMEM((ns, di), F32)],
        compiler_params=pltpu.CompilerParams(vmem_limit_bytes=40 * 1024 * 1024),
        cost_estimate=pl.CostEstimate(
            flops=2 * tokens * di * 1024, bytes_accessed=tokens * 4 * 4000, transcendentals=tokens * 3000
        ),
    )(proj, dyn, aux, seg_rows, filt, bias, head, chan, spread)


def run_backward(
    heads, di, ns, proj, dyn, pre, y, states, aux, aux2, seg_rows, filt, head, chan, spread
):
    tokens, width = proj.shape
    count = tokens // T
    conv = di + 2 * ns
    row = lambda w: pl.BlockSpec((T, w), lambda i: (count - 1 - i, 0))
    return pl.pallas_call(
        functools.partial(backward_kernel, heads, di, ns),
        grid=(count,),
        in_specs=[
            row(width), row(di), row(conv), row(di),
            pl.BlockSpec((1, ns, di), lambda i: (count - 1 - i, 0, 0)),
            row(16), row(2),
            pl.BlockSpec((1, 1, T), lambda i: (count - 1 - i, 0, 0)),
            whole(filt.shape), whole(head.shape), whole(chan.shape), whole(spread.shape),
        ],
        out_specs=[row(width), whole((8, conv)), whole((8, di)), whole((8, 128))],
        out_shape=[
            jax.ShapeDtypeStruct((tokens, width), BF16),
            jax.ShapeDtypeStruct((8, conv), F32),
            jax.ShapeDtypeStruct((8, di), F32),
            jax.ShapeDtypeStruct((8, 128), F32),
        ],
        scratch_shapes=[pltpu.VMEM((T + 8, conv), F32), pltpu.VMEM((ns, di), F32)],
        compiler_params=pltpu.CompilerParams(vmem_limit_bytes=40 * 1024 * 1024),
        cost_estimate=pl.CostEstimate(
            flops=4 * tokens * di * 1024, bytes_accessed=tokens * 4 * 4000, transcendentals=tokens * 4000
        ),
    )(proj, dyn, pre, y, states, aux, aux2, seg_rows, filt, head, chan, spread)


def token_masks(segments):
    seg = segments.reshape(-1, SEQ_LEN)
    count, length = seg.shape
    blocks = seg.reshape(count, length // T, T)
    last = blocks[:, :, -1:]
    before = jnp.pad(last, ((0, 0), (1, 0), (0, 0)), constant_values=-1)[:, :-1]
    columns = [seg, (blocks == before).reshape(seg.shape), (blocks == last).reshape(seg.shape)]
    for k in range(1, 4):
        moved = jnp.pad(seg, ((0, 0), (k, 0)), constant_values=-1)[:, :-k]
        columns.append(moved == seg)
    for k in range(1, 4):
        moved = jnp.pad(seg, ((0, 0), (0, k)), constant_values=-1)[:, k:]
        columns.append(moved == seg)
    columns = [c.astype(F32).reshape(-1) for c in columns]
    columns += [jnp.zeros_like(columns[0])] * (16 - len(columns))
    return jnp.stack(columns, 1), seg.astype(F32).reshape(-1, 1, T)


def shards(
    hidden_in, segments, cotangent, w_z, w_x, w_bc, w_dt, w_out, norm_gain,
    conv_x, bias_x, conv_bc, bias_bc, gate_gain, dt_bias, a_log, d_skip,
):
    dp = lax.axis_size("dp")
    tp = lax.axis_size("tensor")
    own_rows, width = hidden_in.shape
    di = w_z.shape[1]
    heads = w_dt.shape[1]
    ns = w_bc.shape[1] // 2
    per = di // heads
    shard = w_z.shape[0]
    channels = di * tp

    hidden_all = lax.all_gather(hidden_in, "tensor", axis=0, tiled=True)
    small_parts = [norm_gain, conv_x, bias_x, conv_bc, bias_bc, gate_gain]
    small = lax.all_gather(jnp.concatenate([p.reshape(-1) for p in small_parts]), "dp")
    w_local = jnp.concatenate(
        [w_z, w_x, w_bc, w_dt, jnp.zeros((shard, 128 - heads), BF16), w_out.T], 1
    )
    w_full = lax.all_gather(w_local, "dp", axis=0, tiled=True)
    cot_all = lax.all_gather(cotangent, "tensor", axis=0, tiled=True)
    in_width = 2 * di + 2 * ns + 128
    w_in = w_full[:, :in_width]
    w_out_t = w_full[:, in_width:]
    out_all = lax.all_gather(w_out_t, "tensor", axis=0)

    small = small.astype(F32)
    fields, at = [], 0
    for p in small_parts:
        fields.append(small[:, at : at + p.size].reshape((dp,) + p.shape))
        at += p.size
    gain_in = fields[0].reshape(-1)
    filter_x = jnp.transpose(fields[1], (1, 2, 0, 3)).reshape(4, di)
    shift_x = jnp.transpose(fields[2], (1, 0, 2)).reshape(1, di)
    filter_bc = jnp.transpose(fields[3], (1, 0, 2)).reshape(4, 2 * ns)
    shift_bc = fields[4].reshape(1, 2 * ns)
    gain_gate = jnp.transpose(fields[5], (1, 0, 2)).reshape(1, di)
    filt = jnp.concatenate([filter_x, filter_bc], 1)
    bias = jnp.concatenate([shift_x, shift_bc], 1)
    rate = -jnp.exp(a_log)
    head = jnp.pad(jnp.stack([dt_bias, rate]), ((0, 6), (0, 128 - heads)))
    chan = jnp.concatenate([jnp.repeat(d_skip, per)[None], gain_gate, jnp.zeros((6, di), F32)], 0)
    spread = (jnp.arange(128)[:, None] == jnp.arange(di)[None, :] // per).astype(BF16)
    aux, seg_rows = token_masks(segments)

    full = hidden_all.astype(F32)
    inv_full = lax.rsqrt(jnp.mean(full * full, -1, keepdims=True) + EPSILON)
    normed = (full * inv_full * gain_in).astype(BF16)
    proj = mm(normed, w_in)
    dyn = mm(cot_all, w_out_t)
    pre, y, v_low, states, stats = run_forward(
        heads, di, ns, proj, dyn, aux, seg_rows, filt, bias, head, chan, spread
    )
    v_own = lax.all_to_all(v_low, "tensor", split_axis=0, concat_axis=1, tiled=True)
    sums = lax.psum(jnp.stack([stats[:, 0].reshape(-1), stats[:, 4].reshape(-1)]), "tensor")
    inv_gate = lax.rsqrt(sums[0] / channels + EPSILON)
    slope = inv_gate * inv_gate * inv_gate * sums[1] / channels
    aux2 = jnp.stack([inv_gate, slope], 1)
    d_all, conv_acc, chan_acc, head_acc = run_backward(
        heads, di, ns, proj, dyn, pre, y, states, aux, aux2, seg_rows, filt, head, chan, spread
    )
    resid = hidden_in.astype(F32)
    me = lax.axis_index("tensor")
    inv_own = lax.dynamic_slice_in_dim(inv_gate, me * own_rows, own_rows)[:, None]
    out_rows = sum(mm_nt(v_own[:, r * di : (r + 1) * di], out_all[r]) for r in range(tp))
    block_out = (resid + inv_own * out_rows).astype(BF16)

    scaled = (v_low.astype(F32) * inv_gate[:, None]).astype(BF16)
    grad_out = lax.psum_scatter(mm_tn(cot_all, scaled), "dp", scatter_dimension=0, tiled=True)
    d_part = mm_nt(d_all, w_in)
    d_rows = lax.psum_scatter(d_part, "tensor", scatter_dimension=0, tiled=True)
    grad_in = lax.psum_scatter(mm_tn(normed, d_all), "dp", scatter_dimension=0, tiled=True)

    inv_in = lax.rsqrt(jnp.mean(resid * resid, -1, keepdims=True) + EPSILON)
    grad_gain_part = jnp.sum(d_rows * resid * inv_in, 0)
    weighted = d_rows * gain_in
    grad_hidden = (
        cotangent.astype(F32)
        + inv_in * weighted
        - resid * inv_in**3 * jnp.mean(weighted * resid, -1, keepdims=True)
    )

    def by_owner(value, axis):
        shape = value.shape
        cut = value.reshape(shape[:axis] + (dp, shape[axis] // dp) + shape[axis + 1 :])
        return jnp.moveaxis(cut, axis, 0).reshape(dp, -1)

    head_part = jnp.concatenate(
        [
            head_acc[0, :heads],
            rate * head_acc[1, :heads],
            jnp.sum(chan_acc[1].reshape(heads, per), 1),
        ]
    )
    packed = jnp.concatenate(
        [
            by_owner(grad_gain_part, 0),
            by_owner(conv_acc[:4, di:], 1),
            by_owner(conv_acc[4, di:], 0),
            by_owner(conv_acc[:4, :di].reshape(4, heads, per), 2),
            by_owner(conv_acc[4, :di].reshape(heads, per), 1),
            by_owner(chan_acc[0].reshape(heads, per), 1),
            jnp.broadcast_to(head_part[None], (dp, 3 * heads)),
        ],
        1,
    )
    mine = lax.psum_scatter(packed, "dp", scatter_dimension=0, tiled=True).reshape(-1)
    n_gain, n_conv, n_bias = width // dp, 4 * 2 * ns // dp, 2 * ns // dp
    n_shared = n_gain + n_conv + n_bias
    shared = lax.psum(
        jnp.concatenate([grad_in[:, 2 * di : 2 * di + 2 * ns].reshape(-1), mine[:n_shared]]), "tensor"
    )
    n_bc = shard * 2 * ns
    rest = mine[n_shared:]
    n_x = 4 * di // dp
    n_c = di // dp
    return (
        block_out,
        grad_hidden,
        grad_in[:, :di],
        grad_in[:, di : 2 * di],
        shared[:n_bc].reshape(shard, 2 * ns),
        grad_in[:, 2 * di + 2 * ns : 2 * di + 2 * ns + heads],
        grad_out.T,
        shared[n_bc : n_bc + n_gain],
        rest[:n_x].reshape(4, heads, per // dp),
        rest[n_x : n_x + n_c].reshape(heads, per // dp),
        shared[n_bc + n_gain : n_bc + n_gain + n_conv].reshape(4, n_bias),
        shared[n_bc + n_gain + n_conv :],
        rest[n_x + n_c : n_x + 2 * n_c].reshape(heads, per // dp),
        rest[n_x + 2 * n_c : n_x + 2 * n_c + heads],
        rest[n_x + 2 * n_c + heads : n_x + 2 * n_c + 2 * heads],
        rest[n_x + 2 * n_c + 2 * heads :],
    )


def solution(mesh):
    rows = P(("dp", "tensor"), None)
    specs = (
        P("dp", "tensor"), P("dp", "tensor"), P("dp", None), P("dp", "tensor"),
        P("tensor", "dp"), P("dp"), P(None, "tensor", "dp"), P("tensor", "dp"),
        P(None, "dp"), P("dp"), P("tensor", "dp"), P("tensor"), P("tensor"), P("tensor"),
    )
    return jax.shard_map(
        shards,
        mesh=mesh,
        in_specs=(rows, P("dp"), rows) + specs,
        out_specs=(rows, rows) + specs,
        check_vma=False,
    )
```

time: 1510 us -> 694 us (0.46)
  matrix products: 300 us -> 75.9 us
  other arithmetic: 205 us -> 15.1 us
  blocking collectives: 262 us -> 86.3 us
  local copies, waits for them, and re-layouts: 176 us -> 40.6 us
  waiting for transfers between devices: 480 us -> 367 us
  Pallas kernels: 0 us -> 87.8 us
  loops' own time: 48.6 us -> 0 us
    dot_general x66 -> x9, matrix products: 273 us -> 75.9 us  [the longest x5 27 us: mm_nt(): lax.dot_general(a, b, (((1,), (1,)), ((), ())), preferred_element_type=F32)]
    all_gather x7 -> x0, blocking collectives: 180 us -> none  [the longest x1 32.2 us: shards(): lax.all_gather(w_bc, 'dp', axis=0, tiled=True)]
    reduce_scatter x7 -> x3, waiting for transfers between devices: 387 us -> 248 us  [the longest x1 100 us: shards(): d_rows = lax.psum_scatter(d_part, 'tensor', scatter_dimension=0, tiled=True)]
    pallas_call x0 -> x2, Pallas kernels: none -> 87.8 us  [the longest x1 55.2 us: run_backward(): pl.pallas_call(functools.partial(backward_kernel, heads, di, ns), grid=(c...]
    all_gather x6 -> x4, waiting for transfers between devices: 57 us -> 117 us  [the longest x1 70.6 us: shards(): w_full = lax.all_gather(w_local, 'dp', axis=0, tiled=True)]
    mul x30 -> x1, other arithmetic: 52.1 us -> 0.01 us  [shards(): rate * head_acc[1, :heads]]
    another operation x2 -> x0, loops' own time: 48.6 us -> none  [mixer(): lax.map(jax.checkpoint(one_sequence), (x_conv, bc_conv, step_sizes, doc_r...]
    another operation x42 -> x4, other arithmetic: 47.9 us -> 0.07 us  [the longest x1 0.03 us: shards(): jnp.stack([stats[:, 0].reshape(-1), stats[:, 4].reshape(-1)])]
  transfers between devices with their start and end apart: 16 -> 9, of which waited for: 10 -> 6; matrix products, arithmetic and copies ran while one was open for 21% -> 11% of each run, Pallas kernels for 0% -> 0%
where the time goes in v1:
time: 694 us; the launch traced here: 693 us
  waiting for transfers between devices  367 us (53%)
  Pallas kernels  87.8 us (13%)
  blocking collectives  86.3 us (12%)
  matrix products  75.9 us (11%)
  local copies, waits for them, and re-layouts  40.6 us (6%)
  between operations  15.5 us (2%)
  other arithmetic  15.1 us (2%)
    reduce_scatter x1, waiting for transfers between devices, shards(): d_rows = lax.psum_scatter(d_part, 'tensor', scatter_dimension=0, tiled=True)  100 us
    reduce_scatter x1, waiting for transfers between devices, shards(): lax.psum_scatter(mm_tn(normed, d_all), 'dp', scatter_dimension=0, tiled=T...  82 us
    unnamed x2, blocking collectives  75.9 us
    all_gather x1, waiting for transfers between devices, shards(): w_full = lax.all_gather(w_local, 'dp', axis=0, tiled=True)  70.6 us
    reduce_scatter x1, waiting for transfers between devices, shards(): lax.psum_scatter(mm_tn(cot_all, scaled), 'dp', scatter_dimension=0, tiled...  65.8 us
    pallas_call x1, Pallas kernels, run_backward(): pl.pallas_call(functools.partial(backward_kernel, heads, di, ns), grid=(c...  55.2 us
    all_gather x1, waiting for transfers between devices, shards(): cot_all = lax.all_gather(cotangent, 'tensor', axis=0, tiled=True)  46.2 us
    pallas_call x1, Pallas kernels, run_forward(): pl.pallas_call(functools.partial(forward_kernel, heads, di, ns), grid=(co...  32.6 us
  transfers between devices with their start and end apart: 9, of which 6 were waited for; matrix products, arithmetic and copies ran while one was open for 11% of the time, Pallas kernels for 0%

profile of v1, /device:TPU:0, one launch (start us, length us, event | category | flops | bytes accessed | tf_op | source)
XLA Modules:
  0.0 693.1 jit_solution(14607033375531970164)
XLA Ops:
  7.3 0.7 all-gather.7.cloned.1.call-update
  8.0 1.0 copy.99
  9.1 1.0 copy.100
  10.1 1.0 copy.101
  11.2 0.7 constant_dynamic-update-slice_fusion.1
  11.9 0.9 bitcast_dynamic-update-slice_fusion
  12.8 0.8 copy-done.9
  13.7 0.7 all-gather.11.cloned.1.call-update
  14.8 0.6 fusion.55
  16.2 0.2 dynamic-update-slice
  16.4 38.9 %all-reduce.8 = bf16[5376]{0:T(1024)(128)(2,1)S(1)} all-reduce(bf16[5376]{0:T(1024)(128)(2,1)S(1)} %dynamic-update-slice), channel_id=2, replica_groups=mesh['dp'=8,'tensor'=4] {'dp'}, use_global_device_ids=true, to_apply=%add.8 | all-reduce | flops 5376 | bytes 21504
  55.7 0.2 slice_reduce_fusion.4
  55.9 0.2 fusion.39
  56.2 0.2 stack.28
  56.4 0.5 copy.107.aux_ref
  58.4 0.5 all-gather.7.cloned.1.call-done
  58.8 4.1 fusion
  62.9 70.6 %all-gather.9.cloned.1.call-done = bf16[1024,1920]{0,1:T(8,128)(2,1)} async-done(((bf16[128,1920]{0,1:T(8,128)(2,1)}), bf16[1024,1920]{0,1:T(8,128)(2,1)}) %all-gather.9.cloned.1.call-update) | async-done | bytes 3932176 | tf_op jit(solution)/shard_map/all_gather | solution.py:362
  133.5 46.2 %all-gather.11.cloned.1.call-done = bf16[3072,1024]{1,0:T(8,128)(2,1)} async-done(((bf16[768,1024]{1,0:T(8,128)(2,1)}), bf16[3072,1024]{1,0:T(8,128)(2,1)}) %all-gather.11.cloned.1.call-update) | async-done | bytes 6291472 | tf_op jit(solution)/shard_map/all_gather | solution.py:363
  179.7 9.4 %convolution_bitcast_fusion.dyn_ref = f32[3072,512]{1,0:T(8,128)} fusion(bf16[3072,1024]{1,0:T(8,128)(2,1)} %all-gather.11.cloned.1.call-done, bf16[1024,1920]{0,1:T(8,128)(2,1)} %all-gather.9.cloned.1.call-done), kind=kOutput, calls=%fused_computation.11 | convolution fusion | flops 3221225472 | bytes 13631488 | tf_op jit(solution)/shard_map/dot_general | solution.py:18
  189.1 16.1 %fusion.14.proj_ref = f32[3072,1408]{1,0:T(8,128)} fusion(bf16[1024,1920]{0,1:T(8,128)(2,1)S(1)} %copy-done.10, bf16[3072,1024]{1,0:T(8,128)(2,1)} %all-gather.7.cloned.1.call-done, f32[1024]{0:T(1024)S(1)} %get-tuple-element.118, f32[3072]{0:T(1024)S(1)} %add_rsqrt_fusion), kind=kOutput, calls=%fused_computation.23 | convolution fusion | flops 8870952960 | bytes 26492928 | tf_op jit(solution)/shard_map/dot_general | solution.py:18
  205.1 32.6 %shard_map.288 = (f32[3072,768]{1,0:T(8,128)}, f32[3072,512]{1,0:T(8,128)S(1)}, bf16[3072,512]{1,0:T(8,128)(2,1)S(1)}, bf16[24,128,512]{2,1,0:T(8,128)(2,1)S(1)}, f32[24,8,128]{2,1,0:T(8,128)S(1)}) custom-call(f32[3072,1408]{1,0:T(8,128)} %fusion.14.proj_ref, f32[3072,512]{1,0:T(8,128)} %convolution_bitcast_fusion.dyn_ref, f32[3072,16]{1,0:T(8,128)S(1)} %copy.107.aux_ref, ...), custom_call_target="tpu_custom_call" | custom-call | flops 3221225472 | bytes 49152000 | tf_op jit(solution)/shard_map/pallas_call | solution.py:263
  237.7 2.6 copy-done.1
  240.3 1.7 copy-done.2
  242.0 1.7 copy-done.4
  243.7 10.4 %psum.14 = f32[2,3072]{1,0:T(2,128)S(1)} all-reduce(f32[2,3072]{1,0:T(2,128)S(1)} %pad_maximum_fusion.1), channel_id=1, replica_groups=mesh['dp'=8,'tensor'=4] {'tensor'}, use_global_device_ids=true, to_apply=%region_1.2 | all-reduce | flops 6144 | bytes 49152 | tf_op jit(solution)/shard_map/psum | solution.py:397
  254.2 0.5 copy.110.aux2_ref
  254.7 2.8 copy-done
  257.5 1.9 copy-done.3
  259.3 55.2 %shard_map.289 = (bf16[3072,1408]{1,0:T(8,128)(2,1)}, f32[8,768]{1,0:T(8,128)S(1)}, f32[8,512]{1,0:T(8,128)S(1)}, f32[8,128]{1,0:T(8,128)S(1)}) custom-call(f32[3072,1408]{1,0:T(8,128)} %fusion.14.proj_ref, f32[3072,512]{1,0:T(8,128)S(1)} %copy-done, f32[3072,768]{1,0:T(8,128)} %get-tuple-element.27.pre_ref, f32[3072,512]{1,0:T(8,128)} %copy-done.1, ...), custom_call_target="tpu_custom_call" | custom-call | flops 6442450944 | bytes 49152000 | tf_op jit(solution)/shard_map/pallas_call | solution.py:299
  314.6 15.7 %fusion.16 = f32[1024,1408]{1,0:T(8,128)} fusion(bf16[3072,1408]{1,0:T(8,128)(2,1)} %get-tuple-element.30, bf16[3072,1024]{1,0:T(8,128)(2,1)} %all-gather.7.cloned.1.call-done, f32[1024]{0:T(1024)S(1)} %get-tuple-element.118, f32[3072]{0:T(1024)S(1)} %add_rsqrt_fusion), kind=kOutput, calls=%fused_computation.25 | convolution fusion | flops 8870952960 | bytes 20725760 | tf_op jit(solution)/shard_map/dot_general | solution.py:26
  330.4 16.0 %fusion.12 = f32[3072,1024]{1,0:T(8,128)} fusion(bf16[3072,1408]{1,0:T(8,128)(2,1)} %get-tuple-element.30, bf16[1024,1920]{0,1:T(8,128)(2,1)} %all-gather.9.cloned.1.call-done), kind=kOutput, calls=%fused_computation.21 | convolution fusion | flops 8858370048 | bytes 24117248 | tf_op jit(solution)/shard_map/dot_general | solution.py:22
  346.4 2.4 slice.245
  348.9 1.8 fusion.4
  351.8 2.8 copy.108
  354.6 4.7 all-to-all-start
  359.3 0.3 all-reduce.12.cloned.1.call-start
  359.6 82.0 %reduce-scatter.6.cloned.1.call-done = f32[128,1408]{1,0:T(8,128)} async-done(((f32[1024,1408]{1,0:T(8,128)}), f32[128,1408]{1,0:T(8,128)}) %reduce-scatter.6.cloned.1.call-update) | async-done | bytes 720912 | tf_op jit(solution)/shard_map/reduce_scatter | solution.py:414
  441.6 0.9 slice_bitcast_fusion
  442.6 100.3 %reduce-scatter.4.cloned.1.call-done = f32[768,1024]{1,0:T(8,128)} async-done(((f32[3072,1024]{1,0:T(8,128)}), f32[768,1024]{1,0:T(8,128)}) %reduce-scatter.4.cloned.1.call-update) | async-done | bytes 3145744 | tf_op jit(solution)/shard_map/reduce_scatter | solution.py:413
  542.9 3.5 fusion.9
  546.5 37.1 %all-reduce.9 = f32[8,696]{1,0:T(8,128)S(1)} all-reduce(f32[8,696]{1,0:T(8,128)S(1)} %concatenate.30), channel_id=6, replica_groups=mesh['dp'=8,'tensor'=4] {'dp'}, use_global_device_ids=true, to_apply=%region_8.9.clone | all-reduce | flops 5568 | bytes 44544
  583.6 0.7 dynamic-slice_reduce_fusion.1
  584.2 0.7 pad_maximum_fusion
  585.0 7.7 %fusion.19 = f32[1024,512]{0,1:T(8,128)} fusion(bf16[3072,1024]{1,0:T(8,128)(2,1)} %all-gather.11.cloned.1.call-done, bf16[3072,512]{1,0:T(8,128)(2,1)S(1)} %copy-done.5, f32[3072]{0:T(1024)S(1)} %bitcast.121), kind=kOutput, calls=%fused_computation.26 | convolution fusion | flops 3225944064 | bytes 11546624 | tf_op jit(solution)/shard_map/dot_general | solution.py:26
  592.8 2.6 fusion.23
  595.5 2.2 fusion.25
  597.7 2.3 fusion.21
  600.0 4.0 fusion.3
  604.0 0.7 copy.115
  604.6 1.9 fusion.51
  606.5 0.7 dynamic-slice_reduce_fusion.2
  607.2 0.7 reshape.304
  607.9 0.7 dynamic-slice_reduce_fusion.3
  608.7 0.7 reshape.305
  609.3 0.7 reshape.307
  610.0 1.2 dynamic-slice_bitcast_fusion
  611.3 4.4 fusion.6
  615.7 0.9 slice.265
  616.6 0.7 reshape.303
  617.3 1.3 fusion.52
  618.6 0.7 reshape.306
  619.2 1.2 slice.269
  620.4 65.8 %reduce-scatter.8.cloned.1.call-done = f32[128,512]{0,1:T(8,128)} async-done(((f32[1024,512]{0,1:T(8,128)}), f32[128,512]{0,1:T(8,128)}) %reduce-scatter.8.cloned.1.call-update) | async-done | bytes 262160 | tf_op jit(solution)/shard_map/reduce_scatter | solution.py:411
  (142 shorter events, 4.5 us)
Async XLA Ops:
  7.2 7.6 %copy-start.13 = (u32[32]{0:T(128)S(1)}, u32[32]{0:T(128)}, u32[]{:S(2)}) copy-start(u32[32]{0:T(128)} %constant.70) | copy-start | bytes 388
  7.2 7.2 %copy-start.11 = (s32[3072]{0:T(1024)S(1)}, s32[3072]{0:T(1024)}, u32[]{:S(2)}) copy-start(s32[3072]{0:T(1024)} %param.18) | copy-start | bytes 36868
  7.2 7.2 %copy-start.12 = (bf16[4,8,8]{2,1,0:T(8,128)(2,1)S(1)}, bf16[4,8,8]{2,1,0:T(8,128)(2,1)}, u32[]{:S(2)}) copy-start(bf16[4,8,8]{2,1,0:T(8,128)(2,1)} %param.26) | copy-start | bytes 1540
  7.2 7.3 %copy-start.14 = (bf16[8,8]{1,0:T(8,128)(2,1)S(1)}, bf16[8,8]{1,0:T(8,128)(2,1)}, u32[]{:S(2)}) copy-start(bf16[8,8]{1,0:T(8,128)(2,1)} %param.27) | copy-start | bytes 388
  7.2 7.4 %copy-start.20 = (bf16[4,32]{1,0:T(4,128)(2,1)S(1)}, bf16[4,32]{1,0:T(4,128)(2,1)}, u32[]{:S(2)}) copy-start(bf16[4,32]{1,0:T(4,128)(2,1)} %param.28) | copy-start | bytes 772
  7.2 7.5 %copy-start.15 = (bf16[8,8]{1,0:T(8,128)(2,1)S(1)}, bf16[8,8]{1,0:T(8,128)(2,1)}, u32[]{:S(2)}) copy-start(bf16[8,8]{1,0:T(8,128)(2,1)} %param.30) | copy-start | bytes 388
  7.2 8.8 %copy-start.16 = (bf16[128]{0:T(256)(128)(2,1)S(1)}, bf16[128]{0:T(256)(128)(2,1)}, u32[]{:S(2)}) copy-start(bf16[128]{0:T(256)(128)(2,1)} %param.25) | copy-start | bytes 772
  7.3 8.8 %copy-start.17 = (bf16[32]{0:T(256)(128)(2,1)S(1)}, bf16[32]{0:T(256)(128)(2,1)}, u32[]{:S(2)}) copy-start(bf16[32]{0:T(256)(128)(2,1)} %param.29) | copy-start | bytes 196
  7.3 51.6 %all-gather.7.cloned.1.call-start = ((), (), s32[]{:S(2)}) async-start(), calls=%async_computation.4 | async-start | bytes 7864320 | tf_op jit(solution)/shard_map/all_gather | solution.py:356
  8.0 125.5 %all-gather.9.cloned.1.call-start = ((), (), s32[]{:S(2)}) async-start(), calls=%async_computation.5 | async-start | bytes 4423680 | tf_op jit(solution)/shard_map/all_gather | solution.py:362
  11.1 46.8 %copy-start.18 = (f32[8]{0:T(128)S(1)}, f32[8]{0:T(128)}, u32[]{:S(2)}) copy-start(f32[8]{0:T(128)} %param.33) | copy-start | bytes 100
  11.1 47.1 %copy-start.21 = (f32[8]{0:T(128)S(1)}, f32[8]{0:T(128)}, u32[]{:S(2)}) copy-start(f32[8]{0:T(128)} %param.32) | copy-start | bytes 100
  11.2 47.1 %copy-start.19 = (f32[8]{0:T(128)S(1)}, f32[8]{0:T(128)}, u32[]{:S(2)}) copy-start(f32[8]{0:T(128)} %param.31) | copy-start | bytes 100
  12.8 0.8 copy-start.9
  13.6 166.1 %all-gather.11.cloned.1.call-start = ((), (), s32[]{:S(2)}) async-start(), calls=%async_computation.6 | async-start | bytes 7864320 | tf_op jit(solution)/shard_map/all_gather | solution.py:363
  14.3 427.2 %reduce-scatter.6.cloned.1.call-start = ((), (), s32[]{:S(2)}) async-start(), calls=%async_computation.8 | async-start | bytes 6488064 | tf_op jit(solution)/shard_map/reduce_scatter | solution.py:414
  179.7 9.4 %copy-start.10 = (bf16[1024,1920]{0,1:T(8,128)(2,1)S(1)}, bf16[1024,1920]{0,1:T(8,128)(2,1)}, u32[]{:S(2)}) copy-start(bf16[1024,1920]{0,1:T(8,128)(2,1)} %all-gather.9.cloned.1.call-done) | copy-start | bytes 11796484
  237.7 2.6 copy-start.1
  240.3 1.7 copy-start.2
  242.0 1.7 copy-start.4
  254.7 2.8 copy-start
  257.5 1.9 copy-start.3
  330.3 212.6 %reduce-scatter.4.cloned.1.call-start = ((), (), s32[]{:S(2)}) async-start(), calls=%async_computation.7 | async-start | bytes 15728640 | tf_op jit(solution)/shard_map/reduce_scatter | solution.py:413
  346.4 5.5 copy-start.5
  346.4 246.4 %all-gather.13.cloned.1.call-start = ((), (), s32[]{:S(2)}) async-start(), calls=%async_computation.11 | async-start | bytes 5242880 | tf_op jit(solution)/shard_map/all_gather | solution.py:367
  354.6 238.1 %all-to-all-start = ((bf16[4,768,512]{1,2,0:T(8,128)(2,1)}), bf16[4,768,512]{1,2,0:T(8,128)(2,1)}, u32[]{:S(2)}, u32[]{:S(2)}) async-start(bf16[4,768,512]{1,2,0:T(8,128)(2,1)} %copy.108), calls=%async_computation | async-start | bytes 6291456 | tf_op jit(solution)/shard_map/all_to_all | solution.py:396
  359.3 256.4 %all-reduce.12.cloned.1.call-start = ((), (), s32[]{:S(2)}) async-start(), calls=%async_computation.9 | async-start | bytes 270336 | tf_op jit(solution)/shard_map/psum | solution.py:452
  584.9 101.4 %reduce-scatter.8.cloned.1.call-start = ((), (), s32[]{:S(2)}) async-start(), calls=%async_computation.10 | async-start | bytes 2359296 | tf_op jit(solution)/shard_map/reduce_scatter | solution.py:411
  592.8 2.7 copy-start.8
  597.7 2.3 copy-start.6
  600.0 4.0 slice-start
  600.0 11.3 %copy-start.7 = (bf16[768,1024]{1,0:T(8,128)(2,1)S(1)}, bf16[768,1024]{1,0:T(8,128)(2,1)}, u32[]{:S(2)}) copy-start(bf16[768,1024]{1,0:T(8,128)(2,1)} %param.19) | copy-start | bytes 4718596
Sparse Core Ops, SparseCore 0:
  9.7 49.1 all-gather.6
  61.4 72.0 all-gather.8
  135.1 44.5 all-gather.10
  330.4 111.1 reduce-scatter.5
  444.0 98.8 reduce-scatter.3
  544.9 34.4 all-gather.12
  585.0 26.6 all-reduce.11
  616.2 70.0 reduce-scatter.7
